TPU v7x, 128 devices: a whole 4x4x4 slice. The times are simulated.
128 devices in a mesh: gx: 8 (over x, z_hi), gy: 16 (over z_lo, y, core).
Axes of the slice: x: 4, y: 4, z: 4 (z_hi: 2, z_lo: 2; z = z_hi * 2 + z_lo), core: 2. Of those that a mesh axis runs over, the one named last changes fastest.
Arguments:
- layer_input: bfloat16 [1024, 18432], P('gy', 'gx'), may hold values from -480 to 480
- ln_gain: float32 [18432], P('gx'), may hold values from 0.5 to 2
- w_query: bfloat16 [18432, 12288], P('gx', 'gy'), may hold values from -0.046875 to 0.046875
- w_keyval: bfloat16 [18432, 512], P('gx', 'gy'), may hold values from -0.046875 to 0.046875
- w_output: bfloat16 [12288, 18432], P('gy', 'gx'), may hold values from -0.4375 to 0.4375
- kv_cache: bfloat16 [1024, 2048, 512], P(('gx', 'gy')), may hold values from -150 to 150
- lengths: int32 [1024], P(('gx', 'gy')), may hold values from 1 to 2048, as said below
Outputs:
- attn_out: bfloat16 [1024, 18432], P('gy', 'gx')
Inputs may be any that keep to these rules, and one draw needn't show every extreme that they name: `lengths`: slots at and beyond a row's length are ignored; some row has exactly 2048.
All inputs are finite; a program needn't handle non-finite values.
Results may differ from a plain program's by a relative error of at most 0.04.
Values may be sent and summed in bfloat16 or wider, within the bound.
A program may use at most 128 MiB of HBM per device.

v0:
```python
import jax
import jax.numpy as jnp
from jax import lax
from jax.sharding import PartitionSpec as P

HQ = 48
HS = 256


def attend(queries, new_kv, cache_rows, live_lengths):
    row_count = queries.shape[0]
    factor = HS ** (-0.5)
    query_heads = queries.reshape(row_count, HQ, HS)
    cached_keys = cache_rows[:, :, :HS]
    cached_values = cache_rows[:, :, HS:]
    scores = (
        jnp.einsum("rhd,rcd->rhc", query_heads, cached_keys, preferred_element_type=jnp.float32)
        * factor
    )
    valid = (
        lax.broadcasted_iota(jnp.int32, (row_count, 1, cache_rows.shape[1]), 2)
        < live_lengths[:, None, None]
    )
    scores = jnp.where(valid, scores, jnp.float32(-1e30))
    own_score = (
        jnp.einsum("rhd,rd->rh", query_heads, new_kv[:, :HS], preferred_element_type=jnp.float32)
        * factor
    )
    highest = jnp.maximum(jnp.max(scores, axis=-1), own_score)
    probs = jnp.exp(scores - highest[..., None])
    own_prob = jnp.exp(own_score - highest)
    denominator = jnp.sum(probs, axis=-1) + own_prob
    weights = (probs / denominator[..., None]).astype(jnp.bfloat16)
    own_weight = lax.optimization_barrier((own_prob / denominator).astype(jnp.bfloat16)).astype(
        jnp.float32
    )
    mixed = jnp.einsum("rhc,rcd->rhd", weights, cached_values, preferred_element_type=jnp.float32)
    mixed = mixed + own_weight[..., None] * new_kv[:, None, HS:].astype(jnp.float32)
    return mixed.astype(jnp.bfloat16).reshape(row_count, HQ * HS)


def local(layer_input, ln_gain, w_query, w_keyval, w_output, kv_cache, lengths):
    input_f32 = layer_input.astype(jnp.float32)
    feature_count = layer_input.shape[1] * lax.axis_size("gx")
    row_sums, row_squares = lax.psum(
        (
            jnp.sum(input_f32, axis=1, keepdims=True),
            jnp.sum(input_f32 * input_f32, axis=1, keepdims=True),
        ),
        "gx",
    )
    average = row_sums / feature_count
    variance = row_squares / feature_count - average * average
    normed = ((input_f32 - average) * lax.rsqrt(variance + 1e-05) * ln_gain[None, :]).astype(
        jnp.bfloat16
    )
    gathered = lax.all_gather(normed, "gy", axis=0, tiled=True)
    query_part = jnp.dot(gathered, w_query, preferred_element_type=jnp.float32)
    keyval_part = jnp.dot(gathered, w_keyval, preferred_element_type=jnp.float32)
    query_sum, keyval_sum = (
        lax.psum_scatter(
            query_part.astype(jnp.bfloat16), "gx", scatter_dimension=0, tiled=True
        ).astype(jnp.float32),
        lax.psum_scatter(
            keyval_part.astype(jnp.bfloat16), "gx", scatter_dimension=0, tiled=True
        ).astype(jnp.float32),
    )
    query_block = query_sum.astype(jnp.bfloat16)
    keyval_block = keyval_sum.astype(jnp.bfloat16)
    query_mine, keyval_mine = (
        lax.all_to_all(query_block, "gy", split_axis=0, concat_axis=1, tiled=True),
        lax.all_to_all(keyval_block, "gy", split_axis=0, concat_axis=1, tiled=True),
    )
    mixed = attend(query_mine, keyval_mine, kv_cache, lengths)
    head_block = lax.all_to_all(mixed, "gy", split_axis=1, concat_axis=0, tiled=True)
    all_rows = lax.all_gather(head_block, "gx", axis=0, tiled=True)
    return lax.psum_scatter(
        jnp.dot(all_rows, w_output, preferred_element_type=jnp.float32).astype(jnp.bfloat16),
        "gy",
        scatter_dimension=0,
        tiled=True,
    )


def solution(mesh):
    in_specs = (
        P("gy", "gx"),
        P("gx"),
        P("gx", "gy"),
        P("gx", "gy"),
        P("gy", "gx"),
        P(("gx", "gy"), None, None),
        P(("gx", "gy")),
    )
    out_specs = P("gy", "gx")
    return jax.shard_map(local, mesh=mesh, in_specs=in_specs, out_specs=out_specs, check_vma=False)
```

profile of v0, /device:TPU:32, one launch (start us, length us, event | category | flops | bytes accessed | tf_op | source)
XLA Modules:
  0.0 393.9 jit_solution(11738502964025536106)
XLA Ops:
  6.5 0.0 copy-start
  6.5 0.0 all-gather.3.cloned.1.call-start
  6.5 1.3 convert_reduce_fusion
  7.8 24.1 %all-reduce = (f32[64,1]{0,1:T(1,128)S(1)}, f32[64,1]{0,1:T(1,128)S(1)}) all-reduce(f32[64,1]{0,1:T(1,128)S(1)} %bitcast.33, f32[64,1]{0,1:T(1,128)S(1)} %bitcast.32), channel_id=1, replica_groups=mesh['gx'=8,'gy'=16] {'gx'}, use_global_device_ids=true, to_apply=%region_3.0 | all-reduce | flops 128 | bytes 1024 | tf_op jit(solution)/shard_map/psum | solution.py:45
  32.0 1.9 fusion.17
  33.8 0.0 all-gather.3.cloned.1.call-update
  33.9 0.0 reduce-scatter.10.cloned.1.call-start
  33.9 35.5 %all-gather.3.cloned.1.call-done = bf16[1024,2304]{1,0:T(8,128)(2,1)} async-done(((bf16[64,2304]{1,0:T(8,128)(2,1)}), bf16[1024,2304]{1,0:T(8,128)(2,1)}) %all-gather.3.cloned.1.call-update) | async-done | bytes 4718608 | tf_op jit(solution)/shard_map/all_gather | solution.py:57
  69.4 4.4 %convolution_convert_fusion.2 = bf16[1024,32]{0,1:T(8,128)(2,1)} fusion(bf16[1024,2304]{1,0:T(8,128)(2,1)} %all-gather.3.cloned.1.call-done, bf16[2304,32]{0,1:T(8,128)(2,1)} %param.10), kind=kOutput, calls=%fused_computation.14 | convolution fusion | flops 151027712 | bytes 4931584 | tf_op jit(solution)/shard_map/dot_general | solution.py:59
  73.8 1.7 copy.19
  75.5 0.0 reduce-scatter.10.cloned.1.call-update
  75.5 0.0 copy-start.1
  75.5 0.0 reduce-scatter.6.cloned.1.call-start
  75.6 8.4 %convolution_convert_fusion.1 = bf16[1024,768]{1,0:T(8,128)(2,1)} fusion(bf16[1024,2304]{1,0:T(8,128)(2,1)} %all-gather.3.cloned.1.call-done, bf16[2304,768]{1,0:T(8,128)(2,1)} %param.9), kind=kOutput, calls=%fused_computation.9 | convolution fusion | flops 3624665088 | bytes 9830400 | tf_op jit(solution)/shard_map/dot_general | solution.py:58
  84.0 0.0 reduce-scatter.6.cloned.1.call-update
  84.0 61.6 %reduce-scatter.10.cloned.1.call-done = bf16[128,32]{1,0:T(8,128)(2,1)} async-done(((bf16[1024,32]{1,0:T(8,128)(2,1)}), bf16[128,32]{1,0:T(8,128)(2,1)}) %reduce-scatter.10.cloned.1.call-update) | async-done | bytes 8208 | tf_op jit(solution)/shard_map/reduce_scatter | solution.py:64
  145.6 1.4 reshape.44
  147.1 5.7 %all-to-all-start.1 = ((bf16[16,2,128]{2,1,0:T(2,128)(2,1)}), bf16[16,2,128]{2,1,0:T(2,128)(2,1)S(1)}, u32[]{:S(2)}, u32[]{:S(2)}) async-start(bf16[16,2,128]{2,1,0:T(2,128)(2,1)} %reshape.44), calls=%async_computation.2 | async-start | bytes 16384 | tf_op jit(solution)/shard_map/all_to_all | solution.py:72
  152.8 0.0 copy-done.1
  152.8 0.7 iota_compare_fusion
  153.5 3.9 all-to-all-done.1
  157.4 0.7 reshape.45
  158.1 1.4 copy.15
  159.5 0.9 all_to_all.46
  160.4 62.6 %reduce-scatter.6.cloned.1.call-done = bf16[128,768]{1,0:T(8,128)(2,1)} async-done(((bf16[1024,768]{1,0:T(8,128)(2,1)}), bf16[128,768]{1,0:T(8,128)(2,1)}) %reduce-scatter.6.cloned.1.call-update) | async-done | bytes 196624 | tf_op jit(solution)/shard_map/reduce_scatter | solution.py:61
  223.0 5.8 %all-to-all-start = ((bf16[16,8,768]{2,1,0:T(8,128)(2,1)}), bf16[16,8,768]{2,1,0:T(8,128)(2,1)}, u32[]{:S(2)}, u32[]{:S(2)}) async-start(bf16[16,8,768]{2,1,0:T(8,128)(2,1)} %bitcast.27), calls=%async_computation.1 | async-start | bytes 393216 | tf_op jit(solution)/shard_map/all_to_all | solution.py:71
  228.8 0.0 all-gather.5.cloned.1.call-start
  228.8 0.6 slice_convert_fusion
  229.4 5.2 %all-to-all-done = bf16[16,8,768]{2,1,0:T(8,128)(2,1)} async-done(((bf16[16,8,768]{2,1,0:T(8,128)(2,1)}), bf16[16,8,768]{2,1,0:T(8,128)(2,1)}, u32[]{:S(2)}, u32[]{:S(2)}) %all-to-all-start) | async-done | bytes 196640 | tf_op jit(solution)/shard_map/all_to_all | solution.py:71
  234.6 1.6 copy.13
  236.2 1.7 reshape.39
  237.9 1.1 fusion.19
  239.0 6.2 %fusion.22 = (f32[8,48]{1,0:T(8,128)S(1)}, f32[8,48,2048]{2,1,0:T(8,128)S(1)}) fusion(bf16[8,48,256]{2,1,0:T(8,128)(2,1)} %reshape.39, bf16[8,2048,512]{2,1,0:T(8,128)(2,1)} %param.12, pred[8,2048]{1,0:T(8,128)(4,1)} %iota_compare_fusion), kind=kOutput, calls=%fused_computation.33 | convolution fusion | flops 405012096 | bytes 11748864 | tf_op jit(solution)/shard_map/rhd,rcd->rhc/dot_general | solution.py:17
  245.2 0.6 fusion.6
  245.8 5.6 %fusion.12 = bf16[8,48,256]{2,1,0:T(8,128)(2,1)} fusion(bf16[8,2048,512]{2,1,0:T(8,128)(2,1)} %param.12, f32[8,48,2048]{2,1,0:T(8,128)S(1)} %get-tuple-element.16, f32[8,48]{1,0:T(8,128)S(1)} %get-tuple-element.10, f32[8,48]{1,0:T(8,128)S(1)} %multiply_maximum_fusion, f32[8,256]{1,0:T(8,128)S(1)} %get-tuple-element.11, f32[8,48]{1,0:T(8,128)S(1)} %convert_element_type.41), kind=kOutput, calls=%fused_computation.13 | convolution fusion | flops 405307392 | bytes 11743744 | tf_op jit(solution)/shard_map/rhc,rcd->rhd/dot_general | solution.py:37
  251.4 1.7 all_to_all.47
  253.1 1.0 copy.16
  254.1 10.3 %all_to_all.54 = bf16[8,16,768]{2,0,1:T(8,128)(2,1)} all-to-all(bf16[8,16,768]{2,0,1:T(8,128)(2,1)S(1)} %copy.16), channel_id=1, replica_groups=mesh['gx'=8,'gy'=16] {'gy'}, dimensions={1} | all-to-all | bytes 393216 | tf_op jit(solution)/shard_map/all_to_all | solution.py:75
  264.4 0.0 all-gather.5.cloned.1.call-update
  264.4 0.0 reduce-scatter.8.cloned.1.call-start
  264.5 48.9 %all-gather.5.cloned.1.call-done = bf16[1024,768]{1,0:T(8,128)(2,1)} async-done(((bf16[128,768]{1,0:T(8,128)(2,1)}), bf16[1024,768]{1,0:T(8,128)(2,1)}) %all-gather.5.cloned.1.call-update) | async-done | bytes 1572880 | tf_op jit(solution)/shard_map/all_gather | solution.py:76
  313.4 0.0 copy-done
  313.4 7.3 %convolution_convert_fusion = bf16[1024,2304]{1,0:T(8,128)(2,1)} fusion(bf16[1024,768]{1,0:T(8,128)(2,1)} %all-gather.5.cloned.1.call-done, bf16[768,2304]{1,0:T(8,128)(2,1)S(1)} %copy-done), kind=kOutput, calls=%fused_computation.4 | convolution fusion | flops 3626237952 | bytes 9830400 | tf_op jit(solution)/shard_map/dot_general | solution.py:78
  320.7 0.0 reduce-scatter.8.cloned.1.call-update
  320.8 66.6 %reduce-scatter.8.cloned.1.call-done = bf16[64,2304]{1,0:T(8,128)(2,1)} async-done(((bf16[1024,2304]{1,0:T(8,128)(2,1)}), bf16[64,2304]{1,0:T(8,128)(2,1)}) %reduce-scatter.8.cloned.1.call-update) | async-done | bytes 294928 | tf_op jit(solution)/shard_map/reduce_scatter | solution.py:77
  (4 shorter events, 0.0 us)
Async XLA Ops:
  6.5 306.9 %copy-start = (bf16[768,2304]{1,0:T(8,128)(2,1)S(1)}, bf16[768,2304]{1,0:T(8,128)(2,1)}, u32[]{:S(2)}) copy-start(bf16[768,2304]{1,0:T(8,128)(2,1)} %param.11) | copy-start | bytes 10616836
  6.5 62.9 %all-gather.3.cloned.1.call-start = ((), (), s32[]{:S(2)}) async-start(), calls=%async_computation.6 | async-start | bytes 5013504 | tf_op jit(solution)/shard_map/all_gather | solution.py:57
  33.9 111.8 %reduce-scatter.10.cloned.1.call-start = ((), (), s32[]{:S(2)}) async-start(), calls=%async_computation.10 | async-start | bytes 294912 | tf_op jit(solution)/shard_map/reduce_scatter | solution.py:64
  75.5 77.3 %copy-start.1 = (s32[8]{0:T(128)S(1)}, s32[8]{0:T(128)}, u32[]{:S(2)}) copy-start(s32[8]{0:T(128)} %param.13) | copy-start | bytes 100
  75.5 147.4 %reduce-scatter.6.cloned.1.call-start = ((), (), s32[]{:S(2)}) async-start(), calls=%async_computation.7 | async-start | bytes 1769472 | tf_op jit(solution)/shard_map/reduce_scatter | solution.py:61
  147.1 10.4 %all-to-all-start.1 = ((bf16[16,2,128]{2,1,0:T(2,128)(2,1)}), bf16[16,2,128]{2,1,0:T(2,128)(2,1)S(1)}, u32[]{:S(2)}, u32[]{:S(2)}) async-start(bf16[16,2,128]{2,1,0:T(2,128)(2,1)} %reshape.44), calls=%async_computation.2 | async-start | bytes 16384 | tf_op jit(solution)/shard_map/all_to_all | solution.py:72
  223.0 11.6 %all-to-all-start = ((bf16[16,8,768]{2,1,0:T(8,128)(2,1)}), bf16[16,8,768]{2,1,0:T(8,128)(2,1)}, u32[]{:S(2)}, u32[]{:S(2)}) async-start(bf16[16,8,768]{2,1,0:T(8,128)(2,1)} %bitcast.27), calls=%async_computation.1 | async-start | bytes 393216 | tf_op jit(solution)/shard_map/all_to_all | solution.py:71
  228.8 84.6 %all-gather.5.cloned.1.call-start = ((), (), s32[]{:S(2)}) async-start(), calls=%async_computation.8 | async-start | bytes 1769472 | tf_op jit(solution)/shard_map/all_gather | solution.py:76
  264.4 122.9 %reduce-scatter.8.cloned.1.call-start = ((), (), s32[]{:S(2)}) async-start(), calls=%async_computation.9 | async-start | bytes 5013504 | tf_op jit(solution)/shard_map/reduce_scatter | solution.py:77
Sparse Core Ops, SparseCore 0:
  34.0 35.3 all-gather.2
  75.7 69.9 reduce-scatter.9
  149.8 73.0 reduce-scatter.5
  264.6 48.8 all-gather.4
  320.9 66.4 reduce-scatter.7
where the time goes:
time: 396 us; the launch traced here: 394 us
  waiting for transfers between devices  284 us (72%)
  blocking collectives  34.5 us (9%)
  matrix products  33 us (8%)
  between operations  13.2 us (3%)
  local copies, waits for them, and re-layouts  12.1 us (3%)
  starting transfers between devices  11.7 us (3%)
  other arithmetic  5.02 us (1%)
    reduce_scatter x1, waiting for transfers between devices, local(): lax.psum_scatter(jnp.dot(all_rows, w_output, preferred_element_type=jnp.f...  66.6 us
    reduce_scatter x1, waiting for transfers between devices, local(): lax.psum_scatter(query_part.astype(jnp.bfloat16), 'gx', scatter_dimension...  62.6 us
    reduce_scatter x1, waiting for transfers between devices, local(): lax.psum_scatter(keyval_part.astype(jnp.bfloat16), 'gx', scatter_dimensio...  61.6 us
    all_gather x1, waiting for transfers between devices, local(): all_rows = lax.all_gather(head_block, 'gx', axis=0, tiled=True)  48.9 us
    all_gather x1, waiting for transfers between devices, local(): gathered = lax.all_gather(normed, 'gy', axis=0, tiled=True)  35.5 us
    psum x1, blocking collectives, local(): lax.psum((jnp.sum(input_f32, axis=1, keepdims=True), jnp.sum(input_f32 *...  24.1 us
    all_to_all x1, blocking collectives, local(): lax.all_to_all(mixed, 'gy', split_axis=1, concat_axis=0, tiled=True)  10.3 us
    dot_general x1, matrix products, local(): query_part = jnp.dot(gathered, w_query, preferred_element_type=jnp.float32)  8.41 us
  transfers between devices with their start and end apart: 7, of which 7 were waited for; matrix products, arithmetic and copies ran while one was open for 3% of the time, Pallas kernels for 0%

commit v1 on v0

v1 whole, which is shorter than its diff:
```python
import functools

import jax
import jax.numpy as jnp
from jax import lax
from jax.experimental import pallas as pl
from jax.experimental.pallas import tpu as pltpu
from jax.sharding import PartitionSpec as P

MESH = pl.DeviceIdType.MESH
F32 = jnp.float32
BF16 = jnp.bfloat16

HQ = 48
HS = 256
D = 18432
FEATURES = 2304
COLS = 768
KV = 32
CACHE = 2048
ROWS = 64
PAIR = 128
HALF = 400
OUT = 2304


class Ring:
    def __init__(self, device, pos, partner):
        self.device, self.pos, self.partner = device, pos, partner

    def near(self, step):
        return self.device(0, step)

    def across(self):
        return self.device(1, 0)


def gather_plan(ring, slot, ref, half, sends, recvs):
    def whole(i, dz, dr, target):
        place = slot(dz, dr)
        return pltpu.make_async_remote_copy(
            ref.at[place], ref.at[place], sends.at[i], recvs.at[i], device_id=target, device_id_type=MESH
        )

    def part(i, dz, dr, h, target):
        place = slot(dz, dr)
        piece = ref.at[place, pl.ds(h * half, half)]
        return pltpu.make_async_remote_copy(
            piece, piece, sends.at[i], recvs.at[i], device_id=target, device_id_type=MESH
        )

    up, down, across = ring.near(1), ring.near(-1), ring.across()
    outgoing = [
        lambda: whole(0, 0, 0, across),
        lambda: whole(1, 0, 0, up),
        lambda: whole(2, 0, 0, down),
        lambda: whole(3, 1, 0, up),
        lambda: whole(4, 1, 0, down),
        lambda: part(5, 0, -1, 0, up),
        lambda: part(6, 0, 1, 1, down),
        lambda: part(7, 1, -1, 0, up),
        lambda: part(8, 1, 1, 1, down),
    ]
    incoming = [
        lambda: whole(0, 1, 0, across),
        lambda: whole(1, 0, -1, up),
        lambda: whole(2, 0, 1, down),
        lambda: whole(3, 1, -1, up),
        lambda: whole(4, 1, 1, down),
        lambda: part(5, 0, 2, 0, up),
        lambda: part(6, 0, 2, 1, down),
        lambda: part(7, 1, 2, 0, up),
        lambda: part(8, 1, 2, 1, down),
    ]
    return outgoing, incoming


def arrival(s):
    dz = jnp.where((s == 1) | (s == 4) | (s == 5) | (s == 7), 1, 0)
    dr = jnp.where((s == 2) | (s == 4), 3, jnp.where((s == 3) | (s == 5), 1, jnp.where(s >= 6, 2, 0)))
    return dz, dr


class Reduce:
    def __init__(self, ring, mine, part, far, mid, zsend, zrecv, keep, sems):
        self.ring, self.mine, self.part, self.far, self.mid = ring, mine, part, far, mid
        self.zsend, self.zrecv, self.keep = zsend, zrecv, keep
        self.far_send, self.far_recv, self.mid_send, self.mid_recv, self.z_send, self.z_recv = sems

    def role(self, r):
        return lax.rem(r - self.ring.pos + 4, 4)

    def far_copy(self, k, h):
        target = self.ring.near(1 - 2 * h)
        return pltpu.make_async_remote_copy(
            self.part(k, h), self.far.at[k], self.far_send.at[k, h], self.far_recv.at[k],
            device_id=target, device_id_type=MESH,
        )

    def mid_copy(self, k, z, d, h, late):
        target = self.ring.near(1 - 2 * d)
        return pltpu.make_async_remote_copy(
            self.part(k, h), self.mid.at[z, d, h], self.mid_send.at[k, late], self.mid_recv.at[z, d, late],
            device_id=target, device_id_type=MESH,
        )

    def z_copy(self):
        return pltpu.make_async_remote_copy(
            self.zsend, self.zrecv, self.z_send, self.z_recv,
            device_id=self.ring.across(), device_id_type=MESH,
        )

    def first(self, k, z, r):
        role = self.role(r)

        @pl.when(role == 2)
        def _():
            self.far_copy(k, 0).start()
            self.far_copy(k, 1).start()

        @pl.when(lax.rem(role, 2) == 1)
        def _():
            d = role // 2
            self.mid_copy(k, z, d, 1 - d, 0).start()

    def second(self, k, z, r):
        role = self.role(r)

        @pl.when(lax.rem(role, 2) == 1)
        def _():
            d = role // 2
            self.far_copy(k, 0).wait_recv()
            piece = self.part(k, d)
            piece[...] = (piece[...].astype(F32) + self.far[k].astype(F32)).astype(BF16)
            self.mid_copy(k, z, d, d, 1).start()

    def third(self, k, z, r):
        role = self.role(r)

        @pl.when(role == 0)
        def _():
            for d in range(2):
                for late in range(2):
                    h = 1 - d if late == 0 else d
                    self.mid_copy(k, z, d, h, late).wait_recv()

            @pl.when(z != self.ring.partner)
            def _():
                for h in range(2):
                    total = self.part(k, h)[...].astype(F32)
                    total += self.mid[z, 0, h].astype(F32) + self.mid[z, 1, h].astype(F32)
                    self.zsend[h] = total.astype(BF16)
                self.z_copy().start()

            @pl.when(z == self.ring.partner)
            def _():
                for h in range(2):
                    total = self.part(k, h)[...].astype(F32)
                    total += self.mid[z, 0, h].astype(F32) + self.mid[z, 1, h].astype(F32)
                    self.keep[h] = total

    def finish(self, k, z, r):
        role = self.role(r)

        @pl.when(role == 2)
        def _():
            self.far_copy(k, 0).wait_send()
            self.far_copy(k, 1).wait_send()

        @pl.when(lax.rem(role, 2) == 1)
        def _():
            d = role // 2
            self.mid_copy(k, z, d, 1 - d, 0).wait_send()
            self.mid_copy(k, z, d, d, 1).wait_send()


def kernel(
    lengths, gain, x_hbm, wq_hbm, wkv_hbm, wo_hbm, kv_hbm, out_ref,
    x_own, xbuf, wq, wkv, wo, kv, stat_send, stats,
    part1, far1, mid1, zsend1, zrecv1, keep1,
    asend, arecv, qf, new_kv, osf, osend, orecv,
    abuf, tbuf, sib, far2, mid2, zsend2, zrecv2, keep2,
    load_sems, stat_ss, stat_rs, ag1_s, ag1_r, core1_s, core1_r,
    fs1, fr1, ms1, mr1, zs1, zr1, a_s, a_r, o_s, o_r, ag2_s, ag2_r,
    core2_s, core2_r, fs2, fr2, ms2, mr2, zs2, zr2,
):
    gx, gy = lax.axis_index("gx"), lax.axis_index("gy")
    x, zh = gx // 2, lax.rem(gx, 2)
    zl, y, c = gy // 8, lax.rem(gy // 2, 4), lax.rem(gy, 2)

    loads = [
        pltpu.make_async_copy(x_hbm, x_own, load_sems.at[0]),
        pltpu.make_async_copy(wq_hbm, wq, load_sems.at[1]),
        pltpu.make_async_copy(wkv_hbm, wkv, load_sems.at[2]),
        pltpu.make_async_copy(kv_hbm, kv, load_sems.at[3]),
        pltpu.make_async_copy(wo_hbm, wo, load_sems.at[4]),
    ]
    for load in loads:
        load.start()

    barrier = pltpu.get_barrier_semaphore()

    def greet_x(i, carry):
        pl.semaphore_signal(barrier, inc=1, device_id=(lax.rem(gx + i, 8), gy), device_id_type=MESH)
        return carry

    def greet_y(i, carry):
        pl.semaphore_signal(barrier, inc=1, device_id=(gx, lax.rem(gy + i, 16)), device_id_type=MESH)
        return carry

    lax.fori_loop(1, 8, greet_x, 0)
    lax.fori_loop(1, 16, greet_y, 0)

    def y_device(dz, dr):
        return (gx, (lax.rem(zl + dz, 2) * 4 + lax.rem(y + dr + 4, 4)) * 2 + c)

    def x_device(dz, dr):
        return (lax.rem(x + dr + 4, 4) * 2 + lax.rem(zh + dz, 2), gy)

    sibling = (gx, gy + 1 - 2 * c)
    y_ring = Ring(y_device, y, zl)
    x_ring = Ring(x_device, x, zh)

    loads[0].wait()
    row = x_own[...].astype(F32)
    sums = jnp.sum(row, axis=1, keepdims=True)
    squares = jnp.sum(row * row, axis=1, keepdims=True)
    lane = lax.broadcasted_iota(jnp.int32, (ROWS, 128), 1)
    tall = jnp.where(lane == 0, sums, jnp.where(lane == 1, squares, 0.0))
    stat_send[...] = jnp.concatenate([tall, tall], axis=0).T[0:8]
    stats[gx] = stat_send[...]

    pl.semaphore_wait(barrier, 22)

    def stat_copy(i):
        return pltpu.make_async_remote_copy(
            stat_send, stats.at[gx], stat_ss.at[i], stat_rs.at[i],
            device_id=(lax.rem(gx + i, 8), gy), device_id_type=MESH,
        )

    def stat_arrived(i):
        return pltpu.make_async_remote_copy(
            stat_send, stats.at[lax.rem(gx - i + 8, 8)], stat_ss.at[i], stat_rs.at[i],
            device_id=(lax.rem(gx + i, 8), gy), device_id_type=MESH,
        )

    def run(f):
        def body(i, carry):
            f(i)
            return carry

        return body

    lax.fori_loop(1, 8, run(lambda i: stat_copy(i).start()), 0)
    lax.fori_loop(1, 8, run(lambda i: stat_arrived(i).wait_recv()), 0)
    total = jnp.sum(stats[...], axis=0)
    wide = jnp.concatenate([total] * 16, axis=0).T
    average = wide[0:ROWS, 0:1] * (1.0 / D)
    variance = wide[0:ROWS, 1:2] * (1.0 / D) - average * average
    row = x_own[...].astype(F32)
    xbuf[gy] = ((row - average) * lax.rsqrt(variance + 1e-05) * gain[...]).astype(BF16)

    def y_slot(dz, dr):
        return y_device(dz, dr)[1]

    out1, in1 = gather_plan(y_ring, y_slot, xbuf, ROWS // 2, ag1_s, ag1_r)

    def core_copy1(i, dz, dr):
        place = y_slot(dz, dr)
        return pltpu.make_async_remote_copy(
            xbuf.at[place], xbuf.at[place], core1_s.at[i], core1_r.at[i], device_id=sibling, device_id_type=MESH
        )

    def core_arrived1(i, dz, dr):
        place = y_slot(dz, dr) + 1 - 2 * c
        return pltpu.make_async_remote_copy(
            xbuf.at[place], xbuf.at[place], core1_s.at[i], core1_r.at[i], device_id=sibling, device_id_type=MESH
        )

    reduce1 = Reduce(
        x_ring, None, lambda k, h: part1.at[k, h], far1, mid1, zsend1, zrecv1, keep1,
        (fs1, fr1, ms1, mr1, zs1.at[0], zr1.at[0]),
    )

    def chip1(s):
        dz, dr = arrival(s)
        k = lax.rem(zl + dz, 2) * 4 + lax.rem(y + dr, 4)
        return dz, dr, k, lax.rem(k, 2), k // 2

    def compute1(s):
        dz, dr, k, z, r = chip1(s)
        core_arrived1(s, dz, dr).wait_recv()
        lhs = xbuf[pl.ds(2 * k, 2)].reshape(PAIR, FEATURES)
        for t in range(3):
            q = jnp.dot(lhs, wq[:, t * 256 : (t + 1) * 256], preferred_element_type=F32).astype(BF16)
            for u in range(2):
                b = 2 * t + u
                part1[k, b // 3, pl.ds((b % 3) * 128, 128)] = q[:, u * 128 : (u + 1) * 128]
        new = jnp.dot(lhs, wkv[...], preferred_element_type=F32)
        packed = jnp.concatenate([new[32 * j : 32 * j + 32] for j in range(4)], axis=1).astype(BF16)
        part1[k, 0, pl.ds(384, 16)] = packed[0:16]
        part1[k, 1, pl.ds(384, 16)] = packed[16:32]
        reduce1.first(k, z, r)

    for i in range(3):
        out1[i]().start()
    core_copy1(0, 0, 0).start()
    loads[1].wait()
    loads[2].wait()

    def step1(s, carry):
        @pl.when(s == 1)
        def _():
            in1[0]().wait_recv()
            out1[3]().start()
            out1[4]().start()
            core_copy1(1, 1, 0).start()
            in1[1]().wait_recv()
            out1[5]().start()
            core_copy1(2, 0, -1).start()
            in1[2]().wait_recv()
            out1[6]().start()
            core_copy1(3, 0, 1).start()

        @pl.when(s == 4)
        def _():
            in1[3]().wait_recv()
            out1[7]().start()
            core_copy1(4, 1, -1).start()
            in1[4]().wait_recv()
            out1[8]().start()
            core_copy1(5, 1, 1).start()

        @pl.when(s == 6)
        def _():
            in1[5]().wait_recv()
            in1[6]().wait_recv()
            core_copy1(6, 0, 2).start()

        @pl.when(s == 7)
        def _():
            in1[7]().wait_recv()
            in1[8]().wait_recv()
            core_copy1(7, 1, 2).start()

        @pl.when(s < 8)
        def _():
            compute1(s)

        @pl.when((s >= 1) & (s < 9))
        def _():
            _, _, k, z, r = chip1(s - 1)
            reduce1.second(k, z, r)

        @pl.when(s >= 2)
        def _():
            _, _, k, z, r = chip1(s - 2)
            reduce1.third(k, z, r)

        return carry

    lax.fori_loop(0, 10, step1, 0)
    reduce1.z_copy().wait_recv()

    final = [keep1[h] + zrecv1[h].astype(F32) for h in range(2)]
    packed = jnp.concatenate([final[0][384:400], final[1][384:400]], axis=0).reshape(4, 8, 128)
    packed = jnp.concatenate([packed] * 4, axis=0)
    pieces = []
    for h in range(2):
        q = [final[h][b * 128 : (b + 1) * 128].reshape(16, 8, 128) for b in range(3)]
        pieces.append(jnp.concatenate(q + [packed], axis=2))
    asend[...] = jnp.concatenate(pieces, axis=1).astype(BF16)
    arecv[gy] = asend[gy]

    def all_to_all(src, dst, ss, rs):
        def copy(i):
            target = lax.rem(gy + i, 16)
            return pltpu.make_async_remote_copy(
                src.at[target], dst.at[gy], ss.at[i], rs.at[i], device_id=(gx, target), device_id_type=MESH
            )

        def arrived(i):
            target = lax.rem(gy + i, 16)
            return pltpu.make_async_remote_copy(
                src.at[target], dst.at[lax.rem(gy - i + 16, 16)], ss.at[i], rs.at[i],
                device_id=(gx, target), device_id_type=MESH,
            )

        lax.fori_loop(1, 16, run(lambda i: copy(i).start()), 0)
        lax.fori_loop(1, 16, run(lambda i: arrived(i).wait_recv()), 0)
        return copy

    a_copy = all_to_all(asend, arecv, a_s, a_r)

    got = arecv[...].astype(F32)
    for b in range(6):
        h, at = b // 3, (b % 3) * 128
        qf[b] = got[:, 8 * h : 8 * h + 8, at : at + 128].reshape(128, 128)
    fresh = got[:, 0:8, 384:512].reshape(128, 128)
    fresh = pltpu.roll(fresh, lax.rem(128 - 32 * (gy // 4), 128), 1)[:, 0:KV]
    for half in range(2):
        new_kv[:, half * HS : (half + 1) * HS] = jnp.concatenate(
            [fresh[8 * (8 * half + g) : 8 * (8 * half + g) + 8] for g in range(8)], axis=1
        )
    loads[3].wait()

    def attend(r, carry):
        lanes = [qf[b, pl.ds(r, 16, stride=8), :] for b in range(6)]
        q = jnp.concatenate([jnp.concatenate(lanes[2 * j : 2 * j + 2], axis=1) for j in range(3)], axis=0)
        fresh_row = new_kv[pl.ds(r, 1), :]
        scores = lax.dot_general(
            q.astype(BF16), kv[r, :, 0:HS], (((1,), (1,)), ((), ())), preferred_element_type=F32
        ) * (HS**-0.5)
        slot = lax.broadcasted_iota(jnp.int32, (HQ, CACHE), 1)
        scores = jnp.where(slot < lengths[r], scores, -1e30)
        own = jnp.sum(q * fresh_row[:, 0:HS], axis=1, keepdims=True) * (HS**-0.5)
        top = jnp.maximum(jnp.max(scores, axis=1, keepdims=True), own)
        probs = jnp.exp(scores - top)
        own_prob = jnp.exp(own - top)
        scale = 1.0 / (jnp.sum(probs, axis=1, keepdims=True) + own_prob)
        weights = (probs * scale).astype(BF16)
        own_weight = (own_prob * scale).astype(BF16).astype(F32)
        mixed = jnp.dot(weights, kv[r, :, HS : 2 * HS], preferred_element_type=F32)
        mixed += own_weight * fresh_row[:, HS : 2 * HS]
        for b in range(6):
            j, at = b // 2, (b % 2) * 128
            osf[b, pl.ds(r, 16, stride=8), :] = mixed[16 * j : 16 * j + 16, at : at + 128]
        return carry

    lax.fori_loop(0, 8, attend, 0)

    result = [jnp.concatenate([osf[3 * h + b].reshape(16, 8, 128) for b in range(3)], axis=2) for h in range(2)]
    osend[...] = jnp.concatenate(result, axis=1).astype(BF16)
    orecv[gy] = osend[gy]
    o_copy = all_to_all(osend, orecv, o_s, o_r)
    back = orecv[...].astype(F32)
    heads = jnp.concatenate([back[:, 0:8].reshape(PAIR, 384), back[:, 8:16].reshape(PAIR, 384)], axis=1)
    abuf[gx] = heads.astype(BF16)

    def x_slot(dz, dr):
        return x_device(dz, dr)[0]

    out2, in2 = gather_plan(x_ring, x_slot, abuf, PAIR // 2, ag2_s, ag2_r)
    reduce2 = Reduce(
        y_ring, None, lambda k, h: tbuf.at[k, c, pl.ds(h * 32, 32)], far2, mid2, zsend2, zrecv2, keep2,
        (fs2, fr2, ms2, mr2, zs2.at[0], zr2.at[0]),
    )

    def core_copy2(k):
        return pltpu.make_async_remote_copy(
            tbuf.at[k, 1 - c], sib.at[k], core2_s.at[k], core2_r.at[k], device_id=sibling, device_id_type=MESH
        )

    def chip2(s):
        dz, dr = arrival(s)
        k = lax.rem(x + dr, 4) * 2 + lax.rem(zh + dz, 2)
        return k, k // 4, lax.rem(k, 4)

    for i in range(3):
        out2[i]().start()
    loads[4].wait()

    def step2(s, carry):
        @pl.when(s == 1)
        def _():
            in2[0]().wait_recv()
            out2[3]().start()
            out2[4]().start()
            in2[1]().wait_recv()
            out2[5]().start()
            in2[2]().wait_recv()
            out2[6]().start()

        @pl.when(s == 4)
        def _():
            in2[3]().wait_recv()
            out2[7]().start()
            in2[4]().wait_recv()
            out2[8]().start()

        @pl.when(s == 6)
        def _():
            in2[5]().wait_recv()
            in2[6]().wait_recv()

        @pl.when(s == 7)
        def _():
            in2[7]().wait_recv()
            in2[8]().wait_recv()

        @pl.when(s < 8)
        def _():
            k, _, _ = chip2(s)
            lhs = abuf[k]
            for t in range(9):
                term = jnp.dot(lhs, wo[:, t * 256 : (t + 1) * 256], preferred_element_type=F32).astype(BF16)
                tbuf[k, 0, :, t * 256 : (t + 1) * 256] = term[0:ROWS]
                tbuf[k, 1, :, t * 256 : (t + 1) * 256] = term[ROWS:PAIR]
            core_copy2(k).start()

        @pl.when((s >= 1) & (s < 9))
        def _():
            k, z, r = chip2(s - 1)
            core_copy2(k).wait_recv()
            tbuf[k, c] = (tbuf[k, c].astype(F32) + sib[k].astype(F32)).astype(BF16)
            reduce2.first(k, z, r)

        @pl.when((s >= 2) & (s < 10))
        def _():
            k, z, r = chip2(s - 2)
            reduce2.second(k, z, r)

        @pl.when(s >= 3)
        def _():
            k, z, r = chip2(s - 3)
            reduce2.third(k, z, r)

        return carry

    lax.fori_loop(0, 11, step2, 0)
    reduce2.z_copy().wait_recv()
    for h in range(2):
        out_ref[pl.ds(h * 32, 32)] = (keep2[h] + zrecv2[h].astype(F32)).astype(BF16)

    lax.fori_loop(1, 8, run(lambda i: stat_copy(i).wait_send()), 0)
    lax.fori_loop(1, 16, run(lambda i: a_copy(i).wait_send()), 0)
    lax.fori_loop(1, 16, run(lambda i: o_copy(i).wait_send()), 0)
    for i in range(9):
        out1[i]().wait_send()
        out2[i]().wait_send()
    reduce1.z_copy().wait_send()
    reduce2.z_copy().wait_send()

    def drain(s, carry):
        dz, dr, k, z, r = chip1(s)
        core_copy1(s, dz, dr).wait_send()
        reduce1.finish(k, z, r)
        k, z, r = chip2(s)
        core_copy2(k).wait_send()
        reduce2.finish(k, z, r)
        return carry

    lax.fori_loop(0, 8, drain, 0)


def local(layer_input, ln_gain, w_query, w_keyval, w_output, kv_cache, lengths):
    any_space = pl.BlockSpec(memory_space=pl.ANY)
    vmem = pl.BlockSpec(memory_space=pltpu.VMEM)
    dma = pltpu.SemaphoreType.DMA
    scratch = [
        pltpu.VMEM((ROWS, FEATURES), BF16),
        pltpu.VMEM((16, ROWS, FEATURES), BF16),
        pltpu.VMEM((FEATURES, COLS), BF16),
        pltpu.VMEM((FEATURES, KV), BF16),
        pltpu.VMEM((COLS, OUT), BF16),
        pltpu.VMEM((8, CACHE, 2 * HS), BF16),
        pltpu.VMEM((8, 128), F32),
        pltpu.VMEM((8, 8, 128), F32),
        pltpu.VMEM((8, 2, HALF, 128), BF16),
        pltpu.VMEM((8, HALF, 128), BF16),
        pltpu.VMEM((2, 2, 2, HALF, 128), BF16),
        pltpu.VMEM((2, HALF, 128), BF16),
        pltpu.VMEM((2, HALF, 128), BF16),
        pltpu.VMEM((2, HALF, 128), F32),
        pltpu.VMEM((16, 16, 512), BF16),
        pltpu.VMEM((16, 16, 512), BF16),
        pltpu.VMEM((6, 128, 128), F32),
        pltpu.VMEM((8, 2 * HS), F32),
        pltpu.VMEM((6, 128, 128), F32),
        pltpu.VMEM((16, 16, 384), BF16),
        pltpu.VMEM((16, 16, 384), BF16),
        pltpu.VMEM((8, PAIR, COLS), BF16),
        pltpu.VMEM((8, 2, ROWS, OUT), BF16),
        pltpu.VMEM((8, ROWS, OUT), BF16),
        pltpu.VMEM((8, ROWS // 2, OUT), BF16),
        pltpu.VMEM((2, 2, 2, ROWS // 2, OUT), BF16),
        pltpu.VMEM((2, ROWS // 2, OUT), BF16),
        pltpu.VMEM((2, ROWS // 2, OUT), BF16),
        pltpu.VMEM((2, ROWS // 2, OUT), F32),
        dma((5,)),
        dma((8,)), dma((8,)),
        dma((9,)), dma((9,)),
        dma((8,)), dma((8,)),
        dma((8, 2)), dma((8,)), dma((8, 2)), dma((2, 2, 2)), dma((1,)), dma((1,)),
        dma((16,)), dma((16,)), dma((16,)), dma((16,)),
        dma((9,)), dma((9,)),
        dma((8,)), dma((8,)),
        dma((8, 2)), dma((8,)), dma((8, 2)), dma((2, 2, 2)), dma((1,)), dma((1,)),
    ]
    return pl.pallas_call(
        kernel,
        name="decode_attention",
        out_shape=jax.ShapeDtypeStruct((ROWS, OUT), BF16),
        in_specs=[pl.BlockSpec(memory_space=pltpu.SMEM), vmem] + [any_space] * 5,
        out_specs=vmem,
        scratch_shapes=scratch,
        compiler_params=pltpu.CompilerParams(
            collective_id=0, has_side_effects=True, vmem_limit_bytes=60 << 20
        ),
        cost_estimate=pl.CostEstimate(flops=8_300_000_000, bytes_accessed=25_000_000, transcendentals=800_000),
    )(lengths, ln_gain.reshape(1, FEATURES), layer_input, w_query, w_keyval, w_output, kv_cache)


def solution(mesh):
    in_specs = (
        P("gy", "gx"),
        P("gx"),
        P("gx", "gy"),
        P("gx", "gy"),
        P("gy", "gx"),
        P(("gx", "gy"), None, None),
        P(("gx", "gy")),
    )
    out_specs = P("gy", "gx")
    return jax.shard_map(local, mesh=mesh, in_specs=in_specs, out_specs=out_specs, check_vma=False)
```

time: 396 us -> 134 us (0.34)
  waiting for transfers between devices: 284 us -> 0 us
  Pallas kernels: 0 us -> 127 us
  blocking collectives: 34.5 us -> 0 us
  matrix products: 33 us -> 0 us
  between operations: 13.2 us -> 0.01 us
  starting transfers between devices: 11.7 us -> 0 us
  local copies, waits for them, and re-layouts: 12.1 us -> 4.97 us
  other arithmetic: 5.02 us -> 0 us
    reduce_scatter x3 -> x0, waiting for transfers between devices: 191 us -> none  [the longest x1 66.6 us: local(): lax.psum_scatter(jnp.dot(all_rows, w_output, preferred_element_type=jnp.f...]
    pallas_call x0 -> x1, Pallas kernels: none -> 127 us  [local(): pl.pallas_call(kernel, name='decode_attention', out_shape=jax.ShapeDtypeS...]
    all_gather x2 -> x0, waiting for transfers between devices: 84.4 us -> none  [the longest x1 48.9 us: local(): all_rows = lax.all_gather(head_block, 'gx', axis=0, tiled=True)]
    dot_general x6 -> x0, matrix products: 33 us -> none  [the longest x1 8.41 us: local(): query_part = jnp.dot(gathered, w_query, preferred_element_type=jnp.float32)]
    psum x1 -> x0, blocking collectives: 24.1 us -> none  [local(): lax.psum((jnp.sum(input_f32, axis=1, keepdims=True), jnp.sum(input_f32 *...]
    all_to_all x2 -> x0, starting transfers between devices: 11.5 us -> none  [the longest x1 5.78 us: local(): lax.all_to_all(query_block, 'gy', split_axis=0, concat_axis=1, tiled=True)]
    all_to_all x1 -> x0, blocking collectives: 10.3 us -> none  [local(): lax.all_to_all(mixed, 'gy', split_axis=1, concat_axis=0, tiled=True)]
    all_to_all x2 -> x0, waiting for transfers between devices: 9.13 us -> none  [the longest x1 5.2 us: local(): lax.all_to_all(query_block, 'gy', split_axis=0, concat_axis=1, tiled=True)]
  transfers between devices with their start and end apart: 7 -> 0, of which waited for: 7 -> 0; matrix products, arithmetic and copies ran while one was open for 3% -> 0% of each run, Pallas kernels for 0% -> 0%
where the time goes in v1:
time: 134 us; the launch traced here: 132 us
  Pallas kernels  127 us (95%)
  local copies, waits for them, and re-layouts  4.97 us (4%)
    pallas_call x1, Pallas kernels, local(): pl.pallas_call(kernel, name='decode_attention', out_shape=jax.ShapeDtypeS...  127 us
    unnamed x2, local copies, waits for them, and re-layouts  3.65 us

profile of v1, /device:TPU:32, one launch (start us, length us, event | category | flops | bytes accessed | tf_op | source)
XLA Modules:
  0.0 131.7 jit_solution(4576341142917557375)
XLA Ops:
  0.0 1.3 reshape.3.gain
  1.3 2.0 %copy.8.wkv_hbm = bf16[2304,32]{1,0:T(8,128)(2,1)} copy(bf16[2304,32]{0,1:T(8,128)(2,1)} %param.10) | data formatting | bytes 294912 | tf_op args[3]
  3.3 126.7 %decode_attention.1 = bf16[64,2304]{1,0:T(8,128)(2,1)} custom-call(s32[8]{0:T(128)} %lengths.1, f32[1,2304]{1,0:T(1,128)} %reshape.3.gain, bf16[64,2304]{1,0:T(8,128)(2,1)} %x_hbm.1, bf16[2304,768]{1,0:T(8,128)(2,1)} %wq_hbm.1, bf16[2304,32]{1,0:T(8,128)(2,1)} %copy.8.wkv_hbm, bf16[768,2304]{1,0:T(8,128)(2,1)} %wo_hbm.1, bf16[8,2048,512]{2,1,0:T(8,128)(2,1)} %kv_hbm.1), custom_call_target="tpu_custom_call" | custom-call | flops 8300000256 | bytes 25000000 | tf_op jit(solution)/shard_map/decode_attention/pallas_call | solution.py:590
  130.0 1.7 %copy.10 = bf16[64,2304]{1,0:T(8,128)(2,1)} copy(bf16[64,2304]{1,0:T(8,128)(2,1)} %decode_attention.1) | data formatting | bytes 589824

commit v2 on v0

v2 whole, which is shorter than its diff:
```python
import functools

import jax
import jax.numpy as jnp
from jax import lax
from jax.experimental import pallas as pl
from jax.experimental.pallas import tpu as pltpu
from jax.sharding import PartitionSpec as P

MESH = pl.DeviceIdType.MESH
F32 = jnp.float32
BF16 = jnp.bfloat16

HQ = 48
HS = 256
D = 18432
FEATURES = 2304
COLS = 768
KV = 32
CACHE = 2048
ROWS = 64
PAIR = 128
HALF = 400
LAST = 144
OUT = 2304


FAR_FIRST = (12, 4, 11, 13, 5, 3, 10, 14, 6, 2, 8, 9, 7, 15, 1)


class Ring:
    def __init__(self, device, pos, partner):
        self.device, self.pos, self.partner = device, pos, partner

    def near(self, step):
        return self.device(0, step)

    def across(self):
        return self.device(1, 0)


def taken(ref, sem):
    pltpu.make_async_copy(ref, ref, sem).wait()


def gather_plan(ring, slot, ref, half, send, recvs):
    def whole(i, dz, dr, target):
        place = slot(dz, dr)
        return pltpu.make_async_remote_copy(
            ref.at[place], ref.at[place], send, recvs.at[i], device_id=target, device_id_type=MESH
        )

    def part(i, dz, dr, h, target):
        place = slot(dz, dr)
        piece = ref.at[place, pl.ds(h * half, half)]
        return pltpu.make_async_remote_copy(
            piece, piece, send, recvs.at[i], device_id=target, device_id_type=MESH
        )

    up, down, across = ring.near(1), ring.near(-1), ring.across()
    outgoing = [
        lambda: part(0, 0, 0, 0, across),
        lambda: part(1, 0, 0, 1, across),
        lambda: whole(2, 0, 0, up),
        lambda: whole(3, 0, 0, down),
        lambda: part(4, 1, 0, 0, up),
        lambda: part(5, 1, 0, 0, down),
        lambda: part(6, 1, 0, 1, up),
        lambda: part(7, 1, 0, 1, down),
        lambda: part(8, 0, -1, 0, up),
        lambda: part(9, 0, 1, 1, down),
        lambda: part(10, 1, -1, 0, up),
        lambda: part(11, 1, 1, 1, down),
    ]
    incoming = [
        lambda: part(0, 1, 0, 0, across),
        lambda: part(1, 1, 0, 1, across),
        lambda: whole(2, 0, -1, up),
        lambda: whole(3, 0, 1, down),
        lambda: part(4, 1, -1, 0, up),
        lambda: part(5, 1, 1, 0, down),
        lambda: part(6, 1, -1, 1, up),
        lambda: part(7, 1, 1, 1, down),
        lambda: part(8, 0, 2, 0, up),
        lambda: part(9, 0, 2, 1, down),
        lambda: part(10, 1, 2, 0, up),
        lambda: part(11, 1, 2, 1, down),
    ]
    return outgoing, incoming


def arrival(s):
    dz = jnp.where((s == 1) | (s == 4) | (s == 5) | (s == 7), 1, 0)
    dr = jnp.where((s == 2) | (s == 4), 3, jnp.where((s == 3) | (s == 5), 1, jnp.where(s >= 6, 2, 0)))
    return dz, dr


class Reduce:
    def __init__(self, ring, part, far, mid, zsend, zrecv, keep, sems):
        self.ring, self.part, self.far, self.mid = ring, part, far, mid
        self.zsend, self.zrecv, self.keep = zsend, zrecv, keep
        self.send, self.far_recv, self.mid_recv, self.z_send, self.z_recv = sems

    def role(self, r):
        return lax.rem(r - self.ring.pos + 4, 4)

    def far_copy(self, k, z, p, h):
        target = self.ring.near(1 - 2 * h)
        return pltpu.make_async_remote_copy(
            self.part(k, p, h), self.far(z, h, p), self.send, self.far_recv.at[z, h, p],
            device_id=target, device_id_type=MESH,
        )

    def mid_copy(self, k, z, p, d, h):
        target = self.ring.near(1 - 2 * d)
        return pltpu.make_async_remote_copy(
            self.part(k, p, h), self.mid(z, d, p, h), self.send, self.mid_recv.at[z, d, p],
            device_id=target, device_id_type=MESH,
        )

    def z_copy(self, p, h):
        return pltpu.make_async_remote_copy(
            self.zsend(p, h), self.zrecv(p, h), self.z_send, self.z_recv.at[p],
            device_id=self.ring.across(), device_id_type=MESH,
        )

    def first(self, k, z, r, p):
        role = self.role(r)

        @pl.when(role == 2)
        def _():
            self.far_copy(k, z, p, 0).start()
            self.far_copy(k, z, p, 1).start()

        @pl.when(lax.rem(role, 2) == 1)
        def _():
            d = role // 2
            self.mid_copy(k, z, p, d, 1 - d).start()

    def second(self, k, z, r):
        role = self.role(r)

        @pl.when(lax.rem(role, 2) == 1)
        def _():
            d = role // 2
            for p in range(3):
                self.far_copy(k, z, p, d).wait_recv()
                piece = self.part(k, p, d)
                piece[...] = (piece[...].astype(F32) + self.far(z, d, p)[...].astype(F32)).astype(BF16)
                self.mid_copy(k, z, p, d, d).start()

    def third(self, k, z, r):
        role = self.role(r)

        def total(p, h):
            sums = self.mid(z, 0, p, h)[...].astype(F32) + self.mid(z, 1, p, h)[...].astype(F32)
            return self.part(k, p, h)[...].astype(F32) + sums

        @pl.when(role == 0)
        def _():
            for p in range(3):
                for d in range(2):
                    taken(self.mid(z, d, p, None), self.mid_recv.at[z, d, p])

                @pl.when(z != self.ring.partner)
                def _():
                    for h in range(2):
                        self.zsend(p, h)[...] = total(p, h).astype(BF16)
                        self.z_copy(p, h).start()

                @pl.when(z == self.ring.partner)
                def _():
                    for h in range(2):
                        self.keep(p, h)[...] = total(p, h)

    def result(self, p):
        taken(self.zrecv(p, None), self.z_recv.at[p])
        return [self.keep(p, h)[...] + self.zrecv(p, h)[...].astype(F32) for h in range(2)]

    def finish(self, six_blocks, one_block):
        taken(six_blocks, self.send)
        taken(one_block, self.z_send)


def run(f):
    def body(i, carry):
        f(i)
        return carry

    return body


def loop(start, stop, f):
    lax.fori_loop(start, stop, run(f), 0)


def to_columns(rows):
    return jnp.concatenate([rows] * 16, axis=0).T


def kernel(
    lengths_hbm, gain_hbm, x_hbm, wq_hbm, wkv_hbm, wo_hbm, kv_hbm, out_hbm,
    lengths, gain, out,
    xbuf, lhs, wq, wkv, wo, kv, stat_send, stats, row_stats,
    part1, far1, mid1, zsend1, zrecv1, keep1,
    asend, arecv, qf, new_kv, scores, osf, osend, orecv,
    abuf, tbuf, sib, far2, mid2, zsend2, zrecv2, keep2,
    load_sems, out_sems, stat_s, stat_r, row_s, row_r, ag1_s, ag1_r, core1_s, core1_r,
    send1, far1_r, mid1_r, z1_s, z1_r, a_s, a_r, o_s, o_r, ag2_s, ag2_r, core2_s, core2_r,
    send2, far2_r, mid2_r, z2_s, z2_r,
):
    gx, gy = lax.axis_index("gx"), lax.axis_index("gy")
    x, zh = gx // 2, lax.rem(gx, 2)
    zl, y, c = gy // 8, lax.rem(gy // 2, 4), lax.rem(gy, 2)

    loads = [
        pltpu.make_async_copy(x_hbm, xbuf.at[gy], load_sems.at[0]),
        pltpu.make_async_copy(wq_hbm, wq, load_sems.at[1]),
        pltpu.make_async_copy(wkv_hbm, wkv, load_sems.at[2]),
        pltpu.make_async_copy(kv_hbm, kv, load_sems.at[3]),
        pltpu.make_async_copy(wo_hbm, wo, load_sems.at[4]),
        pltpu.make_async_copy(gain_hbm, gain, load_sems.at[5]),
        pltpu.make_async_copy(lengths_hbm, lengths, load_sems.at[6]),
    ]
    loads[0].start()

    barrier = pltpu.get_barrier_semaphore()

    def greet(target):
        pl.semaphore_signal(barrier, inc=1, device_id=target, device_id_type=MESH)

    loop(1, 8, lambda i: greet((lax.rem(gx + i, 8), gy)))
    loop(1, 16, lambda i: greet((gx, lax.rem(gy + i, 16))))

    def y_device(dz, dr):
        return (gx, (lax.rem(zl + dz, 2) * 4 + lax.rem(y + dr + 4, 4)) * 2 + c)

    def x_device(dz, dr):
        return (lax.rem(x + dr + 4, 4) * 2 + lax.rem(zh + dz, 2), gy)

    sibling = (gx, gy + 1 - 2 * c)
    y_ring = Ring(y_device, y, zl)
    x_ring = Ring(x_device, x, zh)

    loads[0].wait()
    for load in loads[1:]:
        load.start()
    row = xbuf[gy].astype(F32)
    sums = jnp.sum(row, axis=1, keepdims=True)
    squares = jnp.sum(row * row, axis=1, keepdims=True)
    lane = lax.broadcasted_iota(jnp.int32, (ROWS, 128), 1)
    tall = jnp.where(lane == 0, sums, jnp.where(lane == 1, squares, 0.0))
    stat_send[...] = jnp.concatenate([tall, tall], axis=0).T[0:8]
    stats[gx] = stat_send[...]

    pl.semaphore_wait(barrier, 22)

    def y_slot(dz, dr):
        return y_device(dz, dr)[1]

    out1, in1 = gather_plan(y_ring, y_slot, xbuf, ROWS // 2, ag1_s.at[0], ag1_r)

    def core_copy1(i, dz, dr):
        place = y_slot(dz, dr)
        return pltpu.make_async_remote_copy(
            xbuf.at[place], xbuf.at[place], core1_s.at[0], core1_r.at[i], device_id=sibling, device_id_type=MESH
        )

    def core_arrived1(i, dz, dr):
        place = y_slot(dz, dr) + 1 - 2 * c
        return pltpu.make_async_remote_copy(
            xbuf.at[place], xbuf.at[place], core1_s.at[0], core1_r.at[i], device_id=sibling, device_id_type=MESH
        )

    def stat_copy(i, slot):
        return pltpu.make_async_remote_copy(
            stat_send, stats.at[slot], stat_s.at[0], stat_r.at[0],
            device_id=(lax.rem(gx + i, 8), gy), device_id_type=MESH,
        )

    def row_copy(i, slot):
        return pltpu.make_async_remote_copy(
            row_stats.at[slot], row_stats.at[slot], row_s.at[0], row_r.at[i],
            device_id=(gx, lax.rem(gy + i, 16)), device_id_type=MESH,
        )

    loop(1, 8, lambda i: stat_copy(i, gx).start())
    for i in range(4):
        out1[i]().start()
    core_copy1(0, 0, 0).start()

    taken(stats.at[pl.ds(0, 7)], stat_r.at[0])
    total = jnp.sum(stats[...], axis=0)
    average = total[0:1] * (1.0 / D)
    variance = total[1:2] * (1.0 / D) - average * average
    deviation = lax.rsqrt(variance + 1e-05)
    row_stats[gy] = jnp.concatenate([average, deviation, jnp.zeros((6, 128), F32)], axis=0)
    for i in FAR_FIRST:
        row_copy(i, gy).start()

    def rows1(p):
        return pl.ds(128 * p, LAST if p == 2 else 128)

    def both(h):
        return pl.ds(0, 2) if h is None else h

    reduce1 = Reduce(
        x_ring,
        lambda k, p, h: part1.at[k, h, rows1(p)],
        lambda z, d, p: far1.at[z, d, rows1(p)],
        lambda z, d, p, h: mid1.at[z, d, both(h), rows1(p)],
        lambda p, h: zsend1.at[h, rows1(p)],
        lambda p, h: zrecv1.at[both(h), rows1(p)],
        lambda p, h: keep1.at[h, rows1(p)],
        (send1.at[0], far1_r, mid1_r, z1_s.at[0], z1_r),
    )

    def chip1(s):
        dz, dr = arrival(s)
        k = lax.rem(zl + dz, 2) * 4 + lax.rem(y + dr, 4)
        return k, lax.rem(k, 2), k // 2

    def compute1(s):
        k, z, r = chip1(s)
        dz, dr = arrival(s)
        for u in range(2):
            source = 2 * k + u
            i = lax.rem(gy - source + 16, 16)

            @pl.when(i > 0)
            def _():
                row_copy(i, source).wait_recv()

        core_arrived1(s, dz, dr).wait_recv()
        first_lanes = lax.broadcasted_iota(jnp.int32, (8, 128), 1) < ROWS
        columns = to_columns(jnp.where(first_lanes, row_stats[2 * k], row_stats[2 * k + 1]))
        rows = xbuf[pl.ds(2 * k, 2)].reshape(PAIR, FEATURES).astype(F32)
        lhs[...] = ((rows - columns[:, 0:1]) * columns[:, 1:2] * gain[...].reshape(1, FEATURES)).astype(BF16)
        for p in range(3):
            q = jnp.dot(lhs[...], wq[:, p * 256 : (p + 1) * 256], preferred_element_type=F32).astype(BF16)
            for h in range(2):
                part1[k, h, pl.ds(128 * p, 128)] = q[:, h * 128 : (h + 1) * 128]
            if p == 2:
                new = lax.dot_general(
                    wkv[...], lhs[...], (((1,), (1,)), ((), ())), preferred_element_type=F32
                ).astype(BF16)
                for h in range(2):
                    part1[k, h, pl.ds(384, 16)] = new[16 * h : 16 * h + 16]
            reduce1.first(k, z, r, p)

    in1[0]().wait_recv()
    out1[4]().start()
    out1[5]().start()
    in1[1]().wait_recv()
    out1[6]().start()
    out1[7]().start()
    core_copy1(1, 1, 0).start()
    in1[2]().wait_recv()
    out1[8]().start()
    core_copy1(2, 0, -1).start()
    in1[3]().wait_recv()
    out1[9]().start()
    core_copy1(3, 0, 1).start()
    loads[1].wait()
    loads[2].wait()
    loads[5].wait()

    def second1(s):
        reduce1.second(*chip1(s))

    def third1(s):
        reduce1.third(*chip1(s))

    def step1(s):
        @pl.when(s == 4)
        def _():
            loop(0, 2, second1)
            in1[4]().wait_recv()
            out1[10]().start()
            in1[7]().wait_recv()
            out1[11]().start()
            in1[6]().wait_recv()
            core_copy1(4, 1, -1).start()
            in1[5]().wait_recv()
            core_copy1(5, 1, 1).start()

        @pl.when(s == 6)
        def _():
            loop(2, 4, second1)
            in1[8]().wait_recv()
            in1[9]().wait_recv()
            core_copy1(6, 0, 2).start()
            loop(0, 2, third1)

        @pl.when(s == 7)
        def _():
            loop(2, 4, third1)
            in1[10]().wait_recv()
            in1[11]().wait_recv()
            core_copy1(7, 1, 2).start()
            loop(4, 6, second1)

        compute1(s)

    loop(0, 8, step1)
    loop(6, 8, second1)
    loop(4, 8, third1)

    final = [reduce1.result(p) for p in range(3)]
    blocks = [final[p][h][0:128].reshape(16, 8, 128) for p in range(3) for h in range(2)]
    fresh = jnp.concatenate([final[2][0][128:144], final[2][1][128:144]] * 4, axis=0).T.reshape(16, 8, 128)
    halves = [jnp.concatenate(blocks[3 * h : 3 * h + 3] + [fresh], axis=2) for h in range(2)]
    asend[...] = jnp.concatenate(halves, axis=1).astype(BF16)
    arecv[gy] = asend[gy]

    def all_to_all(src, dst, ss, rs):
        for i in FAR_FIRST:
            target = lax.rem(gy + i, 16)
            pltpu.make_async_remote_copy(
                src.at[target], dst.at[gy], ss, rs, device_id=(gx, target), device_id_type=MESH
            ).start()
        taken(dst.at[pl.ds(0, 15)], rs)

    all_to_all(asend, arecv, a_s.at[0], a_r.at[0])

    got = arecv[...].astype(F32)
    for b in range(6):
        h, at = b // 3, (b % 3) * 128
        qf[b] = got[:, 8 * h : 8 * h + 8, at : at + 128].reshape(128, 128)
    fresh = got[:, 0:8, 384 : 384 + KV]
    for half in range(2):
        new_kv[:, half * HS : (half + 1) * HS] = jnp.concatenate([fresh[8 * half + g] for g in range(8)], axis=1)
    loads[3].wait()
    loads[6].wait()

    def query(r):
        lanes = [qf[b, pl.ds(r, 16, stride=8), :] for b in range(6)]
        return jnp.concatenate([jnp.concatenate(lanes[2 * j : 2 * j + 2], axis=1) for j in range(3)], axis=0)

    for r in range(8):
        scores[r] = lax.dot_general(
            (query(r) * (HS**-0.5)).astype(BF16), kv[r, :, 0:HS], (((1,), (1,)), ((), ())),
            preferred_element_type=F32,
        )
    slot = lax.broadcasted_iota(jnp.int32, (1, CACHE), 1)
    for r in range(8):
        fresh_row = new_kv[r : r + 1, :]
        score = scores[r] + jnp.where(slot < lengths[r], 0.0, -1e30)
        own = jnp.sum(query(r) * fresh_row[:, 0:HS], axis=1, keepdims=True) * (HS**-0.5)
        top = jnp.maximum(jnp.max(score, axis=1, keepdims=True), own)
        probs = jnp.exp(score - top)
        own_prob = jnp.exp(own - top)
        scale = 1.0 / (jnp.sum(probs, axis=1, keepdims=True) + own_prob)
        mixed = jnp.dot(probs.astype(BF16), kv[r, :, HS : 2 * HS], preferred_element_type=F32)
        mixed = (mixed + own_prob * fresh_row[:, HS : 2 * HS]) * scale
        for b in range(6):
            j, at = b // 2, (b % 2) * 128
            osf[b, pl.ds(r, 16, stride=8), :] = mixed[16 * j : 16 * j + 16, at : at + 128]

    result = [jnp.concatenate([osf[3 * h + b].reshape(16, 8, 128) for b in range(3)], axis=2) for h in range(2)]
    osend[...] = jnp.concatenate(result, axis=1).astype(BF16)
    orecv[gy] = osend[gy]
    all_to_all(osend, orecv, o_s.at[0], o_r.at[0])
    back = orecv[...].astype(F32)
    heads = jnp.concatenate([back[:, 0:8].reshape(PAIR, 384), back[:, 8:16].reshape(PAIR, 384)], axis=1)
    abuf[gx] = heads.astype(BF16)

    def x_slot(dz, dr):
        return x_device(dz, dr)[0]

    out2, in2 = gather_plan(x_ring, x_slot, abuf, PAIR // 2, ag2_s.at[0], ag2_r)
    reduce2 = Reduce(
        y_ring,
        lambda k, p, h: tbuf.at[k, p, c, pl.ds(h * 32, 32)],
        lambda z, d, p: far2.at[z, d, p],
        lambda z, d, p, h: mid2.at[z, d, p, both(h)],
        lambda p, h: zsend2.at[p, h],
        lambda p, h: zrecv2.at[p, both(h)],
        lambda p, h: keep2.at[p, h],
        (send2.at[0], far2_r, mid2_r, z2_s.at[0], z2_r),
    )

    def core_copy2(k, p):
        return pltpu.make_async_remote_copy(
            tbuf.at[k, p, 1 - c], sib.at[k, p], core2_s.at[0], core2_r.at[k, p],
            device_id=sibling, device_id_type=MESH,
        )

    same = jnp.where(x // 2 == zl, 1, 0)
    twin = jnp.where(lax.rem(x, 2) == 0, 1, 3)

    def chip2(s):
        near = jnp.where((s == 3) | (s == 7), twin, 4 - twin)
        dr_same = jnp.where(s < 2, 0, jnp.where((s == 5) | (s == 6), 2, near))
        dz_same = jnp.where((s == 1) | (s == 4) | (s >= 6), 1, 0)
        near = jnp.where((s == 2) | (s == 4), twin, 4 - twin)
        dr_else = jnp.where(s < 2, 0, jnp.where(s >= 6, 2, near))
        dz_else = jnp.where((s == 1) | (s == 4) | (s == 5) | (s == 7), 1, 0)
        dr = same * dr_same + (1 - same) * dr_else
        dz = same * dz_same + (1 - same) * dz_else
        k = lax.rem(x + dr, 4) * 2 + lax.rem(zh + dz, 2)
        return k, k // 4, lax.rem(k, 4)

    for i in range(4):
        out2[i]().start()
    loads[4].wait()

    def first2(s):
        k, z, r = chip2(s)
        for p in range(3):
            core_copy2(k, p).wait_recv()
            tbuf[k, p, c] = (tbuf[k, p, c].astype(F32) + sib[k, p].astype(F32)).astype(BF16)
            reduce2.first(k, z, r, p)

    def second2(s):
        reduce2.second(*chip2(s))

    def third2(s):
        reduce2.third(*chip2(s))

    def step2(s):
        @pl.when(s == 1)
        def _():
            first2(0)
            in2[0]().wait_recv()
            out2[4]().start()
            out2[5]().start()
            in2[1]().wait_recv()
            out2[6]().start()
            out2[7]().start()
            in2[2]().wait_recv()
            out2[8]().start()
            in2[3]().wait_recv()
            out2[9]().start()

        @pl.when(s == 4)
        def _():
            first2(3)
            second2(0)
            in2[4]().wait_recv()
            out2[10]().start()
            in2[7]().wait_recv()
            out2[11]().start()
            in2[6]().wait_recv()
            in2[5]().wait_recv()

        @pl.when(s == 6 - same)
        def _():
            in2[8]().wait_recv()
            in2[9]().wait_recv()

        @pl.when(s == 7 - same)
        def _():
            in2[10]().wait_recv()
            in2[11]().wait_recv()

        k, _, _ = chip2(s)
        rows = abuf[k]
        for p in range(3):
            for t in range(3):
                at = (3 * p + t) * 256
                term = jnp.dot(rows, wo[:, at : at + 256], preferred_element_type=F32).astype(BF16)
                tbuf[k, p, 0, :, t * 256 : (t + 1) * 256] = term[0:ROWS]
                tbuf[k, p, 1, :, t * 256 : (t + 1) * 256] = term[ROWS:PAIR]
            core_copy2(k, p).start()

        @pl.when((s > 1) & (s != 4))
        def _():
            first2(s - 1)

        @pl.when(s >= 4)
        def _():
            second2(s - 3)

        @pl.when(s == 7)
        def _():
            loop(0, 2, third2)

    loop(0, 8, step2)
    first2(7)
    loop(5, 8, second2)
    loop(2, 8, third2)
    writes = []
    for p in range(3):
        for h, rows in enumerate(reduce2.result(p)):
            out[pl.ds(h * 32, 32), p * 768 : (p + 1) * 768] = rows.astype(BF16)
        columns = pl.ds(p * 768, 768)
        writes.append(pltpu.make_async_copy(out.at[:, columns], out_hbm.at[:, columns], out_sems.at[p]))
        writes[p].start()

    taken(stats.at[pl.ds(0, 7)], stat_s.at[0])
    taken(row_stats.at[pl.ds(0, 15)], row_s.at[0])
    taken(asend.at[pl.ds(0, 15)], a_s.at[0])
    taken(osend.at[pl.ds(0, 15)], o_s.at[0])
    taken(xbuf.at[pl.ds(0, 7)], ag1_s.at[0])
    taken(abuf.at[pl.ds(0, 7)], ag2_s.at[0])
    taken(xbuf.at[pl.ds(0, 8)], core1_s.at[0])
    taken(sib, core2_s.at[0])
    reduce1.finish(part1.at[pl.ds(0, 6)], zsend1)
    reduce2.finish(tbuf.at[pl.ds(0, 6), :, 0], zsend2)
    for write in writes:
        write.wait()


def local(layer_input, ln_gain, w_query, w_keyval, w_output, kv_cache, lengths):
    any_space = pl.BlockSpec(memory_space=pl.ANY)
    dma = pltpu.SemaphoreType.DMA
    scratch = [
        pltpu.SMEM((8,), jnp.int32),
        pltpu.VMEM((FEATURES,), F32),
        pltpu.VMEM((ROWS, OUT), BF16),
        pltpu.VMEM((16, ROWS, FEATURES), BF16),
        pltpu.VMEM((PAIR, FEATURES), BF16),
        pltpu.VMEM((FEATURES, COLS), BF16),
        pltpu.VMEM((KV, FEATURES), BF16),
        pltpu.VMEM((COLS, OUT), BF16),
        pltpu.VMEM((8, CACHE, 2 * HS), BF16),
        pltpu.VMEM((8, 128), F32),
        pltpu.VMEM((8, 8, 128), F32),
        pltpu.VMEM((16, 8, 128), F32),
        pltpu.VMEM((8, 2, HALF, 128), BF16),
        pltpu.VMEM((2, 2, HALF, 128), BF16),
        pltpu.VMEM((2, 2, 2, HALF, 128), BF16),
        pltpu.VMEM((2, HALF, 128), BF16),
        pltpu.VMEM((2, HALF, 128), BF16),
        pltpu.VMEM((2, HALF, 128), F32),
        pltpu.VMEM((16, 16, 512), BF16),
        pltpu.VMEM((16, 16, 512), BF16),
        pltpu.VMEM((6, 128, 128), F32),
        pltpu.VMEM((8, 2 * HS), F32),
        pltpu.VMEM((8, HQ, CACHE), F32),
        pltpu.VMEM((6, 128, 128), F32),
        pltpu.VMEM((16, 16, 384), BF16),
        pltpu.VMEM((16, 16, 384), BF16),
        pltpu.VMEM((8, PAIR, COLS), BF16),
        pltpu.VMEM((8, 3, 2, ROWS, 768), BF16),
        pltpu.VMEM((8, 3, ROWS, 768), BF16),
        pltpu.VMEM((2, 2, 3, 32, 768), BF16),
        pltpu.VMEM((2, 2, 3, 2, 32, 768), BF16),
        pltpu.VMEM((3, 2, 32, 768), BF16),
        pltpu.VMEM((3, 2, 32, 768), BF16),
        pltpu.VMEM((3, 2, 32, 768), F32),
        dma((7,)), dma((3,)),
        dma((1,)), dma((1,)), dma((1,)), dma((16,)),
        dma((1,)), dma((12,)), dma((1,)), dma((8,)),
        dma((1,)), dma((2, 2, 3)), dma((2, 2, 3)), dma((1,)), dma((3,)),
        dma((1,)), dma((1,)), dma((1,)), dma((1,)),
        dma((1,)), dma((12,)), dma((1,)), dma((8, 3)),
        dma((1,)), dma((2, 2, 3)), dma((2, 2, 3)), dma((1,)), dma((3,)),
    ]
    return pl.pallas_call(
        kernel,
        name="decode_attention",
        out_shape=jax.ShapeDtypeStruct((ROWS, OUT), BF16),
        in_specs=[any_space] * 7,
        out_specs=any_space,
        scratch_shapes=scratch,
        compiler_params=pltpu.CompilerParams(
            collective_id=0, has_side_effects=True, vmem_limit_bytes=60 << 20
        ),
        cost_estimate=pl.CostEstimate(flops=8_300_000_000, bytes_accessed=25_000_000, transcendentals=800_000),
    )(lengths, ln_gain, layer_input, w_query, w_keyval.T, w_output, kv_cache)


def solution(mesh):
    in_specs = (
        P("gy", "gx"),
        P("gx"),
        P("gx", "gy"),
        P("gx", "gy"),
        P("gy", "gx"),
        P(("gx", "gy"), None, None),
        P(("gx", "gy")),
    )
    out_specs = P("gy", "gx")
    return jax.shard_map(local, mesh=mesh, in_specs=in_specs, out_specs=out_specs, check_vma=False)
```

time: 396 us -> 103 us (0.26)
  the two profiles are of different devices: /device:TPU:32 before, /device:TPU:34 now
where the time goes in v2:
time: 103 us
  Pallas kernels  101 us (98%)
  local copies, waits for them, and re-layouts  1.69 us (2%)
    pallas_call x1, Pallas kernels, local(): pl.pallas_call(kernel, name='decode_attention', out_shape=jax.ShapeDtypeS...  101 us

profile of v2, /device:TPU:34, one launch (start us, length us, event | category | flops | bytes accessed | tf_op | source)
XLA Modules:
  0.0 102.8 jit_solution(1644476676361496124)
XLA Ops:
  0.0 101.1 %decode_attention.1 = bf16[64,2304]{1,0:T(8,128)(2,1)} custom-call(s32[8]{0:T(128)} %lengths_hbm.1, f32[2304]{0:T(1024)} %gain_hbm.1, bf16[64,2304]{1,0:T(8,128)(2,1)} %x_hbm.1, bf16[2304,768]{1,0:T(8,128)(2,1)} %wq_hbm.1, bf16[32,2304]{1,0:T(8,128)(2,1)} %bitcast.1, bf16[768,2304]{1,0:T(8,128)(2,1)} %wo_hbm.1, bf16[8,2048,512]{2,1,0:T(8,128)(2,1)} %kv_hbm.1), custom_call_target="tpu_custom_call" | custom-call | flops 8300000256 | bytes 25000000 | tf_op jit(solution)/shard_map/decode_attention/pallas_call | solution.py:651
  101.1 1.7 %copy.9 = bf16[64,2304]{1,0:T(8,128)(2,1)} copy(bf16[64,2304]{1,0:T(8,128)(2,1)} %decode_attention.1) | data formatting | bytes 589824

commit v3 on v2

--- a/solution.py
+++ b/solution.py
@@ -374,7 +374,6 @@
     def step1(s):
         @pl.when(s == 4)
         def _():
-            loop(0, 2, second1)
             in1[4]().wait_recv()
             out1[10]().start()
             in1[7]().wait_recv()
@@ -383,18 +382,17 @@
             core_copy1(4, 1, -1).start()
             in1[5]().wait_recv()
             core_copy1(5, 1, 1).start()
+            loop(0, 2, second1)
 
         @pl.when(s == 6)
         def _():
-            loop(2, 4, second1)
             in1[8]().wait_recv()
             in1[9]().wait_recv()
             core_copy1(6, 0, 2).start()
-            loop(0, 2, third1)
+            loop(2, 4, second1)
 
         @pl.when(s == 7)
         def _():
-            loop(2, 4, third1)
             in1[10]().wait_recv()
             in1[11]().wait_recv()
             core_copy1(7, 1, 2).start()
@@ -403,6 +401,7 @@
         compute1(s)
 
     loop(0, 8, step1)
+    loop(0, 4, third1)
     loop(6, 8, second1)
     loop(4, 8, third1)
 
@@ -529,8 +528,11 @@
             out2[6]().start()
             out2[7]().start()
             in2[2]().wait_recv()
+            in2[3]().wait_recv()
+
+        @pl.when(s == 3)
+        def _():
             out2[8]().start()
-            in2[3]().wait_recv()
             out2[9]().start()
 
         @pl.when(s == 4)
@@ -578,15 +580,14 @@
 
     loop(0, 8, step2)
     first2(7)
-    loop(5, 8, second2)
-    loop(2, 8, third2)
+    loop(5, 7, second2)
+    loop(2, 4, third2)
+    second2(7)
+    loop(4, 8, third2)
     writes = []
     for p in range(3):
         for h, rows in enumerate(reduce2.result(p)):
-            out[pl.ds(h * 32, 32), p * 768 : (p + 1) * 768] = rows.astype(BF16)
-        columns = pl.ds(p * 768, 768)
-        writes.append(pltpu.make_async_copy(out.at[:, columns], out_hbm.at[:, columns], out_sems.at[p]))
-        writes[p].start()
+            out_hbm[pl.ds(h * 32, 32), p * 768 : (p + 1) * 768] = rows.astype(BF16)
 
     taken(stats.at[pl.ds(0, 7)], stat_s.at[0])
     taken(row_stats.at[pl.ds(0, 15)], row_s.at[0])
@@ -598,8 +599,6 @@
     taken(sib, core2_s.at[0])
     reduce1.finish(part1.at[pl.ds(0, 6)], zsend1)
     reduce2.finish(tbuf.at[pl.ds(0, 6), :, 0], zsend2)
-    for write in writes:
-        write.wait()
 
 
 def local(layer_input, ln_gain, w_query, w_keyval, w_output, kv_cache, lengths):
@@ -651,9 +650,9 @@
     return pl.pallas_call(
         kernel,
         name="decode_attention",
-        out_shape=jax.ShapeDtypeStruct((ROWS, OUT), BF16),
+        out_shape=pltpu.VMEM((ROWS, OUT), BF16),
         in_specs=[any_space] * 7,
-        out_specs=any_space,
+        out_specs=pl.BlockSpec(memory_space=pltpu.VMEM),
         scratch_shapes=scratch,
         compiler_params=pltpu.CompilerParams(
             collective_id=0, has_side_effects=True, vmem_limit_bytes=60 << 20

time: 103 us -> 97.7 us (0.949)
  the two profiles are of different devices: /device:TPU:34 before, /device:TPU:32 now
where the time goes in v3:
time: 97.7 us; the launch traced here: 97.6 us
  Pallas kernels  96.9 us (99%)
    pallas_call x1, Pallas kernels, local(): pl.pallas_call(kernel, name='decode_attention', out_shape=pltpu.VMEM((ROW...  96.9 us

profile of v3, /device:TPU:32, one launch (start us, length us, event | category | flops | bytes accessed | tf_op | source)
XLA Modules:
  0.0 97.6 jit_solution(8661888563345719502)
XLA Ops:
  0.0 96.9 %decode_attention.1 = bf16[64,2304]{1,0:T(8,128)(2,1)S(1)} custom-call(s32[8]{0:T(128)} %lengths_hbm.1, f32[2304]{0:T(1024)} %gain_hbm.1, bf16[64,2304]{1,0:T(8,128)(2,1)} %x_hbm.1, bf16[2304,768]{1,0:T(8,128)(2,1)} %wq_hbm.1, bf16[32,2304]{1,0:T(8,128)(2,1)} %bitcast.1, bf16[768,2304]{1,0:T(8,128)(2,1)} %wo_hbm.1, bf16[8,2048,512]{2,1,0:T(8,128)(2,1)} %kv_hbm.1), custom_call_target="tpu_custom_call" | custom-call | flops 8300000256 | bytes 25000000 | tf_op jit(solution)/shard_map/decode_attention/pallas_call | solution.py:650
  96.9 0.7 copy.9

commit v4 on v3

--- a/solution.py
+++ b/solution.py
@@ -538,13 +538,13 @@
         @pl.when(s == 4)
         def _():
             first2(3)
-            second2(0)
             in2[4]().wait_recv()
             out2[10]().start()
             in2[7]().wait_recv()
             out2[11]().start()
             in2[6]().wait_recv()
             in2[5]().wait_recv()
+            second2(0)
 
         @pl.when(s == 6 - same)
         def _():

time: 97.7 us -> 97.7 us (level)
  no operation moved by 1% of the time
where the time goes in v4:
time: 97.7 us; the launch traced here: 97.6 us
  Pallas kernels  96.9 us (99%)
    pallas_call x1, Pallas kernels, local(): pl.pallas_call(kernel, name='decode_attention', out_shape=pltpu.VMEM((ROW...  96.9 us

profile of v4, /device:TPU:32, one launch (start us, length us, event | category | flops | bytes accessed | tf_op | source)
XLA Modules:
  0.0 97.6 jit_solution(762795689638968231)
XLA Ops:
  0.0 96.9 %decode_attention.1 = bf16[64,2304]{1,0:T(8,128)(2,1)S(1)} custom-call(s32[8]{0:T(128)} %lengths_hbm.1, f32[2304]{0:T(1024)} %gain_hbm.1, bf16[64,2304]{1,0:T(8,128)(2,1)} %x_hbm.1, bf16[2304,768]{1,0:T(8,128)(2,1)} %wq_hbm.1, bf16[32,2304]{1,0:T(8,128)(2,1)} %bitcast.1, bf16[768,2304]{1,0:T(8,128)(2,1)} %wo_hbm.1, bf16[8,2048,512]{2,1,0:T(8,128)(2,1)} %kv_hbm.1), custom_call_target="tpu_custom_call" | custom-call | flops 8300000256 | bytes 25000000 | tf_op jit(solution)/shard_map/decode_attention/pallas_call | solution.py:650
  96.9 0.7 copy.9
